TPU v7x, 32 devices: a whole 2x2x4 slice. The times are simulated.
32 devices in a mesh: parts: 2 (over y), track: 4 (over z), tm: 2 (over x), coef: 2 (over core).
Axes of the slice: x: 2, y: 2, z: 4, core: 2. Of those that a mesh axis runs over, the one named last changes fastest.
Arguments:
- sector_ids: int32 [12288], P(('parts', 'track', 'tm')), parts along dimension 0, may hold values from 0 to 63, as said below
- observed: float32 [3, 12288], P(None, ('parts', 'track', 'tm')), parts along dimension 1, may hold values from -6 to 6
- weights: float32 [3, 12288], P(None, ('parts', 'track', 'tm')), parts along dimension 1, may hold values from 0.3 to 3
- coefficients: float32 [2048, 128], P(('parts', 'track')), parts along dimension 0, may hold values from -6 to 6
- tile_index: int32 [128, 12], P(('parts', 'track', 'tm'), 'coef'), parts along dimension 0, may hold values from 0 to 1023, as said below
- tile_count: int32 [128], P(('parts', 'track', 'tm')), parts along dimension 0, may hold values from 3 to 12
- sensitivity: bfloat16 [128, 12, 3, 128, 128], P(('parts', 'track', 'tm'), 'coef'), parts along dimension 0, may hold values from -0.15625 to 0.15625
Outputs:
- gradient: float32 [2048, 128], P(('parts', 'track')), parts along dimension 0
There are 2 independent parts, one for each index of `parts`. A program takes and returns all parts, laid end to end along the dimension named above; each array names one. Nothing has to cross between parts.
Inputs may be any that keep to these rules, and one draw needn't show every extreme that they name: `sector_ids`: the rows of one index of track and tm fall in at most 192 rows into the 8 consecutive sectors of any one index, and some pair reaches 192; the sectors of each index receive exactly 768 rows in all; each sector holds at most 128 rows, and every index holds a sector with exactly 128. `tile_index`: entries at positions from tile_count on are arbitrary blocks and take no part. Block n belongs to track index n // 256. Of the 48 entries held by one index of track, tm and coef (its sectors' rows, its coef share of the columns), live or not, at most 24 name blocks of any one track index, and every such device has a track index named exactly 24 times.
All inputs are finite; a program needn't handle non-finite values.
Results may differ from a plain program's by a relative error of at most 0.0037.
Values may be sent and summed in bfloat16 or wider, within the bound.
A program may use at most 64 MiB of HBM per device.

v0:
```python
import jax
import jax.numpy as jnp
from jax import lax
from jax.sharding import PartitionSpec as P

HUBER = 2.0


def per_device(sector_ids, observed, weights, coefficients, tile_index, tile_count, sensitivity):
    sector_total = tile_index.shape[0]
    half_k = tile_index.shape[1]
    slot_count = sensitivity.shape[3]
    block_width = sensitivity.shape[4]
    owners = lax.axis_size(("track", "tm"))
    row_total = sector_ids.shape[0]
    capacity = 2 * row_total // owners
    rounded = coefficients.astype(jnp.bfloat16)
    every_block = lax.all_gather(rounded, "track", axis=0, tiled=True)
    owner_of = sector_ids // sector_total
    local_sector = sector_ids % sector_total
    onehot = (owner_of[:, None] == jnp.arange(owners, dtype=jnp.int32)[None, :]).astype(jnp.int32)
    ranking = jnp.sum((jnp.cumsum(onehot, axis=0) - 1) * onehot, axis=1)
    placing = owner_of * capacity + ranking
    payload = jnp.concatenate([observed, weights], axis=0)
    outgoing = jnp.zeros((6, owners * capacity), jnp.float32).at[:, placing].set(payload)
    outgoing = jnp.transpose(outgoing.reshape(6, owners, capacity), (1, 0, 2))
    labels = jnp.full((owners * capacity,), -1, jnp.int32).at[placing].set(local_sector)
    labels = labels.reshape(owners, capacity)
    got_rows, got_labels = (
        lax.all_to_all(outgoing, ("track", "tm"), split_axis=0, concat_axis=0, tiled=True),
        lax.all_to_all(labels, ("track", "tm"), split_axis=0, concat_axis=0, tiled=True),
    )
    received = jnp.transpose(got_rows, (1, 0, 2)).reshape(6, owners * capacity)
    flat_labels = got_labels.reshape(owners * capacity)
    member = (flat_labels[:, None] == jnp.arange(sector_total, dtype=jnp.int32)[None, :]).astype(
        jnp.int32
    )
    within = jnp.sum((jnp.cumsum(member, axis=0) - 1) * member, axis=1)
    target = jnp.where(
        flat_labels >= 0, flat_labels * slot_count + within, sector_total * slot_count
    )
    gridded = jnp.zeros((6, sector_total * slot_count + 1), jnp.float32).at[:, target].set(received)
    gridded = jnp.transpose(gridded[:, :-1].reshape(6, sector_total, slot_count), (1, 0, 2))
    observed_tiles = gridded[:, :3]
    weight_tiles = gridded[:, 3:]
    k_global = lax.axis_index("coef") * half_k + jnp.arange(half_k, dtype=jnp.int32)
    active = k_global[None, :] < tile_count[:, None]
    blocks = jnp.take(every_block, tile_index, axis=0)
    blocks = jnp.where(active[:, :, None], blocks, jnp.zeros_like(blocks))
    partial_pred = jnp.einsum(
        "skcjb,skb->scj", sensitivity, blocks, preferred_element_type=jnp.float32
    )
    predicted = lax.psum(partial_pred, "coef")
    scaled = weight_tiles * (predicted - observed_tiles)
    force = (weight_tiles * scaled / jnp.sqrt(1.0 + (scaled / HUBER) ** 2)).astype(jnp.bfloat16)
    tile_grad = jnp.einsum("skcjb,scj->skb", sensitivity, force, preferred_element_type=jnp.float32)
    tile_grad = jnp.where(active[:, :, None], tile_grad, jnp.zeros_like(tile_grad))
    block_total = every_block.shape[0]
    partial_grad = jnp.zeros((block_total, block_width), jnp.float32)
    partial_grad = partial_grad.at[tile_index.reshape(-1)].add(tile_grad.reshape(-1, block_width))
    summed = lax.psum_scatter(partial_grad, "track", scatter_dimension=0, tiled=True)
    gradient = lax.psum(summed, ("tm", "coef"))
    return gradient


def solution(mesh):
    placed = (
        P(("parts", "track", "tm")),
        P(None, ("parts", "track", "tm")),
        P(None, ("parts", "track", "tm")),
        P(("parts", "track"), None),
        P(("parts", "track", "tm"), "coef"),
        P(("parts", "track", "tm")),
        P(("parts", "track", "tm"), "coef", None, None, None),
    )
    return jax.shard_map(
        per_device,
        mesh=mesh,
        in_specs=placed,
        out_specs=P(("parts", "track"), None),
        check_vma=False,
    )
```

profile of v0, /device:TPU:0, one launch (start us, length us, event | category | flops | bytes accessed | tf_op | source)
XLA Modules:
  0.0 135.0 jit_solution(9949122944024813271)
XLA Ops:
  6.5 0.7 add_select_fusion
  7.2 1.7 %reduce-window.14 = s32[8,6,128]{2,0,1:T(8,128)S(1)} reduce-window(s32[8,6,128]{2,0,1:T(8,128)S(1)} %fusion.13, s32[]{:T(128)} %constant.40.clone.1), window={size=1x1x128 pad=0_0x0_0x127_0}, to_apply=%region_0.1 | reduce-window | flops 780288 | bytes 49156 | tf_op jit(solution)/shard_map/reduce-window
  9.5 3.4 %scatter_custom_fusion = s32[1536]{0:T(1024)S(1)} fusion(s32[768]{0:T(1024)S(1)} %compare_select_fusion.2, s32[768]{0:T(1024)S(1)} %get-tuple-element.7, s32[]{:T(128)} %constant.74.clone.1), kind=kCustom, calls=%fused_computation.50 | custom fusion | bytes 6148 | tf_op jit(solution)/shard_map/scatter | solution.py:27
  12.9 0.7 all_to_all.9
  13.6 7.3 %all-to-all-start = ((s32[8,1,192]{2,1,0:T(1,128)}), s32[8,1,192]{2,1,0:T(1,128)S(1)}, u32[]{:S(2)}, u32[]{:S(2)}) async-start(s32[8,1,192]{2,1,0:T(1,128)} %all_to_all.9), calls=%async_computation | async-start | bytes 16384 | tf_op jit(solution)/shard_map/all_to_all | solution.py:31
  20.8 0.7 compare_select_fusion.1
  21.5 0.8 reshape.166
  22.3 0.7 maximum_bitcast_fusion
  23.2 4.4 %scatter_custom_fusion.1 = f32[6,1536]{0,1:T(8,128)S(1)} fusion(s32[768]{0:T(1024)S(1)} %compare_select_fusion.2, f32[768,6]{1,0:T(8,128)S(1)} %copy.26, f32[]{:T(128)} %constant.39.clone.1), kind=kCustom, calls=%fused_computation.7 | custom fusion | bytes 36868 | tf_op jit(solution)/shard_map/scatter | solution.py:25
  27.6 1.0 copy.27
  28.6 0.9 convert_element_type.18
  29.5 14.5 %all_gather.3 = bf16[1024,128]{1,0:T(8,128)(2,1)S(1)} all-gather(bf16[256,128]{1,0:T(8,128)(2,1)S(1)} %convert_element_type.18), channel_id=1, replica_groups=mesh['parts'=2,'track'=4,'tm'=2,'coef'=2] {'track'}, dimensions={0}, use_global_device_ids=true | all-gather | bytes 327680 | tf_op jit(solution)/shard_map/all_gather | solution.py:18
  44.7 0.8 compare_and_fusion
  45.5 3.7 %fusion = f32[8,1,3,128,1]{3,1,4,2,0:T(1,128)S(1)} fusion(bf16[8,6,3,128,128]{4,3,2,1,0:T(8,128)(2,1)} %param.13, bf16[8,6,128,1,1]{2,1,0,3,4:T(8,128)(2,1)S(1)} %select_bitcast_fusion), kind=kOutput, calls=%fused_computation.5 | convolution fusion | flops 4718592 | bytes 4743168 | tf_op jit(solution)/shard_map/skcjb,skb->scj/dot_general | solution.py:50
  49.2 3.3 %psum.14 = f32[8,3,128]{2,0,1:T(8,128)S(1)} all-reduce(f32[8,3,128]{2,0,1:T(8,128)S(1)} %bitcast.50), channel_id=1, replica_groups=mesh['parts'=2,'track'=4,'tm'=2,'coef'=2] {'coef'}, use_global_device_ids=true, to_apply=%region_9.10 | all-reduce | flops 3072 | bytes 24576 | tf_op jit(solution)/shard_map/psum | solution.py:53
  52.5 5.7 %all-to-all-start.1 = ((f32[8,6,192]{2,1,0:T(8,128)}), f32[8,6,192]{2,1,0:T(8,128)S(1)}, u32[]{:S(2)}, u32[]{:S(2)}) async-start(f32[8,6,192]{2,1,0:T(8,128)} %bitcast.8), calls=%async_computation.1 | async-start | bytes 131072 | tf_op jit(solution)/shard_map/all_to_all | solution.py:30
  58.5 2.3 %reduce-window.16 = s32[8,12,128]{2,1,0:T(8,128)S(1)} reduce-window(s32[8,12,128]{2,1,0:T(8,128)S(1)} %fusion.8, s32[]{:T(128)} %constant.40.clone.1), window={size=1x1x128 pad=0_0x0_0x127_0}, to_apply=%region_4.5 | reduce-window | flops 1560576 | bytes 98308 | tf_op jit(solution)/shard_map/reduce-window.2
  61.6 3.5 %all-to-all-done.1 = f32[8,6,192]{2,1,0:T(8,128)S(1)} async-done(((f32[8,6,192]{2,1,0:T(8,128)}), f32[8,6,192]{2,1,0:T(8,128)S(1)}, u32[]{:S(2)}, u32[]{:S(2)}) %all-to-all-start.1) | async-done | bytes 36896 | tf_op jit(solution)/shard_map/all_to_all | solution.py:30
  65.5 4.4 %scatter_custom_fusion.2 = f32[6,1025]{0,1:T(8,128)S(1)} fusion(s32[1536]{0:T(1024)S(1)} %fusion.17, f32[1536,6]{1,0:T(8,128)S(1)} %copy.29, f32[]{:T(128)} %constant.39.clone.1), kind=kCustom, calls=%fused_computation.9 | custom fusion | bytes 24604 | tf_op jit(solution)/shard_map/scatter | solution.py:42
  70.2 3.1 %fusion.15 = f32[8,1,6,128,1]{3,1,4,2,0:T(1,128)S(1)} fusion(bf16[8,6,3,128,128]{4,3,2,1,0:T(8,128)(2,1)} %param.13, bf16[8,3,128,1,1]{2,0,1,3,4:T(8,128)(2,1)S(1)} %fusion.18), kind=kOutput, calls=%fused_computation.34 | convolution fusion | flops 4718592 | bytes 4749312 | tf_op jit(solution)/shard_map/skcjb,scj->skb/dot_general | solution.py:56
  73.4 1.5 %scatter_custom_fusion.3 = f32[1024,128]{1,0:T(8,128)} fusion(s32[48]{0:T(128)S(1)} %fusion.23, f32[48,128]{1,0:T(8,128)S(1)} %reshape.209, f32[]{:T(128)} %constant.39.clone.1), kind=kCustom, calls=%fused_computation.11 | custom fusion | flops 6144 | bytes 524292 | tf_op jit(solution)/shard_map/scatter-add | solution.py:60
  75.0 19.6 %reduce-scatter.2.cloned.1.call-done = f32[256,128]{1,0:T(8,128)} async-done(((f32[1024,128]{1,0:T(8,128)}), f32[256,128]{1,0:T(8,128)}) %reduce-scatter.2.cloned.1.call-update) | async-done | bytes 131088 | tf_op jit(solution)/shard_map/reduce_scatter | solution.py:61
  94.7 32.0 %all-reduce.2.cloned.1.call-done = f32[256,128]{1,0:T(8,128)} async-done(((f32[256,128]{1,0:T(8,128)}), f32[256,128]{1,0:T(8,128)}) %all-reduce.2.cloned.1.call-update) | async-done | bytes 131088 | tf_op jit(solution)/shard_map/psum | solution.py:62
  126.6 1.6 %copy.49 = f32[256,128]{1,0:T(8,128)} copy(f32[256,128]{1,0:T(8,128)} %all-reduce.2.cloned.1.call-done) | data formatting | bytes 262144
  (41 shorter events, 3.4 us)
Async XLA Ops:
  13.6 38.9 %all-to-all-start = ((s32[8,1,192]{2,1,0:T(1,128)}), s32[8,1,192]{2,1,0:T(1,128)S(1)}, u32[]{:S(2)}, u32[]{:S(2)}) async-start(s32[8,1,192]{2,1,0:T(1,128)} %all_to_all.9), calls=%async_computation | async-start | bytes 16384 | tf_op jit(solution)/shard_map/all_to_all | solution.py:31
  52.5 12.6 %all-to-all-start.1 = ((f32[8,6,192]{2,1,0:T(8,128)}), f32[8,6,192]{2,1,0:T(8,128)S(1)}, u32[]{:S(2)}, u32[]{:S(2)}) async-start(f32[8,6,192]{2,1,0:T(8,128)} %bitcast.8), calls=%async_computation.1 | async-start | bytes 131072 | tf_op jit(solution)/shard_map/all_to_all | solution.py:30
  58.2 36.4 %reduce-scatter.2.cloned.1.call-start = ((), (), s32[]{:S(2)}) async-start(), calls=%async_computation.3 | async-start | bytes 655360 | tf_op jit(solution)/shard_map/reduce_scatter | solution.py:61
  75.0 51.7 %all-reduce.2.cloned.1.call-start = ((), (), s32[]{:S(2)}) async-start(), calls=%async_computation.4 | async-start | bytes 262144 | tf_op jit(solution)/shard_map/psum | solution.py:62
Sparse Core Ops, SparseCore 0:
  75.1 19.5 reduce-scatter.1
  97.0 29.6 all-reduce.1
where the time goes:
time: 136 us; the launch traced here: 135 us
  waiting for transfers between devices  55.2 us (41%)
  local copies, waits for them, and re-layouts  18.6 us (14%)
  blocking collectives  17.8 us (13%)
  between operations  13.5 us (10%)
  starting transfers between devices  13.1 us (10%)
  other arithmetic  10.2 us (7%)
  matrix products  6.73 us (5%)
    psum x1, waiting for transfers between devices, per_device(): gradient = lax.psum(summed, ('tm', 'coef'))  32 us
    reduce_scatter x1, waiting for transfers between devices, per_device(): lax.psum_scatter(partial_grad, 'track', scatter_dimension=0, tiled=True)  19.6 us
    all_gather x1, blocking collectives, per_device(): every_block = lax.all_gather(rounded, 'track', axis=0, tiled=True)  14.5 us
    all_to_all x1, starting transfers between devices, per_device(): lax.all_to_all(labels, ('track', 'tm'), split_axis=0, concat_axis=0, tile...  7.25 us
    all_to_all x1, starting transfers between devices, per_device(): lax.all_to_all(outgoing, ('track', 'tm'), split_axis=0, concat_axis=0, ti...  5.72 us
    scatter x1, local copies, waits for them, and re-layouts, per_device(): jnp.zeros((6, sector_total * slot_count + 1), jnp.float32).at[:, target]  4.45 us
    scatter x1, local copies, waits for them, and re-layouts, per_device(): jnp.zeros((6, owners * capacity), jnp.float32).at[:, placing].set(payload)  4.36 us
    another operation x4, other arithmetic  4.31 us
  transfers between devices with their start and end apart: 4, of which 3 were waited for; matrix products, arithmetic and copies ran while one was open for 13% of the time, Pallas kernels for 0%

commit v1 on v0

v1 whole, which is shorter than its diff:
```python
import functools

import jax
import jax.numpy as jnp
from jax import lax
from jax.experimental import pallas as pl
from jax.experimental.pallas import tpu as pltpu
from jax.sharding import PartitionSpec as P

HUBER = 2.0
F32 = jnp.float32
BF16 = jnp.bfloat16
NT = (((1,), (1,)), ((), ()))
NN = (((1,), (0,)), ((), ()))


def dot(a, b, dims=NN):
    return lax.dot_general(a, b, dims, preferred_element_type=F32)


def iota(shape, dim):
    return lax.broadcasted_iota(jnp.int32, shape, dim)


def kernel(
    dims, count_ref, sid_ref, obs_ref, wts_ref, coef_ref, tile_ref, sens_hbm, out_ref,
    sens, coefs, rows, preds, gsend, grecv,
    sens_sem, coef_send, coef_recv, row_send, row_recv, pred_send, pred_recv, grad_send, grad_recv,
):
    nt, nm, nc, ns, hk, lr = dims
    owners, total = nt * nm, nt * nm * nc
    slots = 128
    per = coef_ref.shape[0]
    nq = sid_ref.shape[0]
    entries = ns * hk
    t, m, c = lax.axis_index("track"), lax.axis_index("tm"), lax.axis_index("coef")
    own = t * nm + m
    me = own * nc + c

    def place(d):
        return {"track": d // (nm * nc), "tm": (d // nc) % nm, "coef": d % nc}

    sector_rows = hk * 3 * slots
    loads = [
        pltpu.make_async_copy(
            sens_hbm.at[pl.ds(s * sector_rows, sector_rows)],
            sens.at[pl.ds(s * sector_rows, sector_rows)],
            sens_sem.at[s],
        )
        for s in range(ns)
    ]
    barrier = pltpu.get_barrier_semaphore()

    @pl.loop(1, total)
    def _(p):
        pl.semaphore_signal(
            barrier, inc=1, device_id=place((me + p) % total), device_id_type=pl.DeviceIdType.MESH
        )

    for load in loads:
        load.start()
    coefs[pl.ds(pl.multiple_of(t * per, per), per)] = coef_ref[...].astype(BF16)
    for q in range(nq):
        lanes = pl.ds(q * 128, 128)
        rows[own, pl.ds(q * 8, 3)] = obs_ref[:, lanes]
        rows[own, pl.ds(q * 8 + 3, 3)] = wts_ref[:, lanes]
        rows[own, pl.ds(q * 8 + 6, 1)] = sid_ref[pl.ds(q, 1), :].astype(F32)
        rows[own, pl.ds(q * 8 + 7, 1)] = jnp.zeros((1, 128), F32)
    pl.semaphore_wait(barrier, total - 1)

    def coef_copy(p, source):
        other = (t + p) % nt
        at = coefs.at[pl.ds(pl.multiple_of(source * per, per), per)]
        return pltpu.make_async_remote_copy(
            src_ref=at, dst_ref=at, send_sem=coef_send.at[p], recv_sem=coef_recv.at[source],
            device_id={"track": other, "tm": m, "coef": c}, device_id_type=pl.DeviceIdType.MESH,
        )

    def row_copy(p, source):
        other = (own + p) % owners
        return pltpu.make_async_remote_copy(
            src_ref=rows.at[source], dst_ref=rows.at[source],
            send_sem=row_send.at[p], recv_sem=row_recv.at[source],
            device_id={"track": other // nm, "tm": other % nm, "coef": c},
            device_id_type=pl.DeviceIdType.MESH,
        )

    def pred_copy(p, source):
        return pltpu.make_async_remote_copy(
            src_ref=preds.at[source], dst_ref=preds.at[source],
            send_sem=pred_send.at[p], recv_sem=pred_recv.at[source],
            device_id={"track": t, "tm": m, "coef": (c + p) % nc},
            device_id_type=pl.DeviceIdType.MESH,
        )

    def grad_copy(p, source):
        other = (me + p) % total
        first = pl.multiple_of((other // (nm * nc)) * lr, lr)
        return pltpu.make_async_remote_copy(
            src_ref=gsend.at[pl.ds(first, lr)], dst_ref=grecv.at[source],
            send_sem=grad_send.at[p], recv_sem=grad_recv.at[source],
            device_id=place(other), device_id_type=pl.DeviceIdType.MESH,
        )

    @pl.loop(1, nt)
    def _(p):
        coef_copy(p, t).start()

    @pl.loop(1, owners)
    def _(p):
        row_copy(p, own).start()

    index = jnp.concatenate([tile_ref[:, pl.ds(k, 1)] for k in range(hk)], axis=0)
    sub = iota((ns, 1), 0)
    count = jnp.zeros((ns, 1), jnp.int32)
    for s in range(ns):
        count = jnp.where(sub == s, count_ref[s], count)
    active = jnp.concatenate(
        [jnp.where(c * hk + k < count, 1.0, 0.0) for k in range(hk)], axis=0
    )
    pick = jnp.where((iota((entries, nt * per), 1) == index) & (active > 0.5), 1.0, 0.0).astype(BF16)
    lane = iota((entries, 128), 1)
    named = (index >= lane * per) & (index < (lane + 1) * per)
    named_f = jnp.where(named, 1.0, 0.0)
    before = jnp.where(iota((entries, entries), 1) < iota((entries, entries), 0), 1.0, 0.0)
    rank = jnp.sum(dot(before.astype(BF16), named_f.astype(BF16)) * named_f, axis=1, keepdims=True)
    track = jnp.sum(jnp.where(named, lane, 0).astype(F32), axis=1, keepdims=True)
    within = index.astype(F32) - track * per + 1.0
    lane_f = lane.astype(F32)
    shift = (lax.rem(me, 128 // lr) * lr).astype(F32)
    marks = []
    for u in range(nt):
        marks.append(
            jnp.sum(
                jnp.where((track == u) & (rank + shift == lane_f), within, 0.0), axis=0, keepdims=True
            )
        )
    wide = iota((entries, nt * lr), 1).astype(F32)
    squeeze = jnp.where(track * lr + rank == wide, 1.0, 0.0).T.astype(BF16)

    @pl.loop(1, nt)
    def _(p):
        coef_copy(nt - p, (t + p) % nt).wait_recv()

    blocks = dot(pick, coefs[...])
    wide_blocks = jnp.concatenate(
        [blocks[k * ns:(k + 1) * ns] for k in range(hk)], axis=1
    ).astype(BF16)
    pixels = 3 * slots

    def tile(s, k):
        return sens[pl.ds((s * hk + k) * pixels, pixels), :]

    which = iota((ns, pixels), 0)
    pred = jnp.zeros((ns, pixels), F32)
    for s in range(ns):
        loads[s].wait()
        part = dot(wide_blocks, jnp.concatenate([tile(s, k) for k in range(hk)], axis=1), NT)
        pred = jnp.where(which == s, part, pred)
    preds[c] = pred

    @pl.loop(1, nc)
    def _(p):
        pred_copy(p, c).start()

    @pl.loop(1, owners)
    def _(p):
        row_copy(owners - p, (own + p) % owners).wait_recv()

    ri, rj = iota((128, 256), 0), iota((128, 256), 1)
    tri = jnp.where((ri < rj) | (rj >= 128), 1.0, 0.0).astype(BF16)
    sector = (own * ns + iota((ns, 128), 0)).astype(F32)
    slot_at = iota((slots, 128), 0).astype(F32)

    def source_rows(o, carry):
        base, grid = carry
        got = rows[o]
        hits = []
        for q in range(nq):
            hits.append(jnp.where(got[q * 8 + 6:q * 8 + 7] == sector, 1.0, 0.0))
        ahead = dot(jnp.concatenate(hits, axis=0).astype(BF16), tri)
        put, high, low = [], [], []
        for q in range(nq):
            hit = hits[q]
            rank_q = ahead[q * ns:(q + 1) * ns, :128] + base
            base = base + ahead[q * ns:(q + 1) * ns, 128:]
            slot = jnp.sum(hit * rank_q, axis=0, keepdims=True)
            put.append(jnp.where(slot == slot_at, 1.0, 0.0).astype(BF16))
            chunk = jnp.concatenate(
                [hit * got[q * 8 + i:q * 8 + i + 1] for i in range(6)], axis=0
            )
            upper = chunk.astype(BF16)
            high.append(upper)
            low.append((chunk - upper.astype(F32)).astype(BF16))
        put = jnp.concatenate(put, axis=1)
        both = jnp.concatenate(
            [jnp.concatenate(high, axis=1), jnp.concatenate(low, axis=1)], axis=0
        )
        return base, grid + dot(both, put, NT)

    _, grid = lax.fori_loop(
        0, owners, source_rows,
        (jnp.zeros((ns, 128), F32), jnp.zeros((12 * ns, slots), F32)),
    )
    grid = grid[:6 * ns] + grid[6 * ns:]

    @pl.loop(1, nc)
    def _(p):
        pred_copy(nc - p, (c + p) % nc).wait_recv()

    pred = preds[0]
    for i in range(1, nc):
        pred = pred + preds[i]
    forces = []
    for i in range(3):
        w = grid[(3 + i) * ns:(4 + i) * ns]
        scaled = w * (pred[:, i * slots:(i + 1) * slots] - grid[i * ns:(i + 1) * ns])
        forces.append(w * scaled * lax.rsqrt(1.0 + (scaled / HUBER) ** 2))
    force = jnp.concatenate(forces, axis=1).astype(BF16)
    which = iota((ns, hk * 128), 0)
    grad = jnp.zeros((ns, hk * 128), F32)
    for s in range(ns):
        part = dot(force, jnp.concatenate([tile(s, k) for k in range(hk)], axis=1))
        grad = jnp.where(which == s, part, grad)
    grad = jnp.concatenate([grad[:, k * 128:(k + 1) * 128] for k in range(hk)], axis=0)
    grad = jnp.where(active > 0.5, grad, 0.0).astype(BF16)
    packed = dot(squeeze, grad)
    line = iota((nt * lr, 128), 0)
    for u in range(nt):
        packed = jnp.where(line == u * lr + lr - 1, marks[u], packed)
    gsend[...] = packed.astype(BF16)
    grecv[me] = gsend[pl.ds(pl.multiple_of(t * lr, lr), lr)]

    @pl.loop(1, total)
    def _(p):
        grad_copy(p, me).start()

    @pl.loop(1, total)
    def _(p):
        grad_copy(total - p, (me + p) % total).wait_recv()

    together = 128 // lr
    at = iota((per, 128), 0).astype(F32) + 1.0

    def gather_group(g, acc):
        base = g * together
        mark = jnp.zeros((1, 128), F32)
        for i in range(together):
            mark = mark + grecv[base + i].astype(F32)[lr - 1:lr]
        terms = jnp.concatenate([grecv[base + i] for i in range(together)], axis=0)
        return acc + dot(jnp.where(at == mark, 1.0, 0.0).astype(BF16), terms)

    out_ref[...] = lax.fori_loop(0, total // together, gather_group, jnp.zeros((per, 128), F32))

    @pl.loop(1, nt)
    def _(p):
        coef_copy(p, t).wait_send()

    @pl.loop(1, owners)
    def _(p):
        row_copy(p, own).wait_send()

    @pl.loop(1, nc)
    def _(p):
        pred_copy(p, c).wait_send()

    @pl.loop(1, total)
    def _(p):
        grad_copy(p, me).wait_send()


def per_device(sector_ids, observed, weights, coefficients, tile_index, tile_count, sensitivity):
    nt, nm, nc = lax.axis_size("track"), lax.axis_size("tm"), lax.axis_size("coef")
    ns, hk = tile_index.shape
    per, width = coefficients.shape
    nq = sector_ids.shape[0] // 128
    slots = sensitivity.shape[3]
    owners, total = nt * nm, nt * nm * nc
    cap = 2 * ns * hk // nt
    lr = (cap + 1 + 15) // 16 * 16
    flat = ns * hk * 3 * slots
    vmem = pl.BlockSpec(memory_space=pltpu.VMEM)
    dma = pltpu.SemaphoreType.DMA
    return pl.pallas_call(
        functools.partial(kernel, (nt, nm, nc, ns, hk, lr)),
        out_shape=jax.ShapeDtypeStruct((per, width), F32),
        in_specs=[pl.BlockSpec(memory_space=pltpu.SMEM)] + [vmem] * 5
        + [pl.BlockSpec(memory_space=pl.ANY)],
        out_specs=vmem,
        scratch_shapes=[
            pltpu.VMEM((flat, width), BF16),
            pltpu.VMEM((nt * per, width), BF16),
            pltpu.VMEM((owners, nq * 8, 128), F32),
            pltpu.VMEM((nc, ns, 3 * slots), F32),
            pltpu.VMEM((nt * lr, width), BF16),
            pltpu.VMEM((total, lr, width), BF16),
            dma((ns,)),
            dma((nt,)), dma((nt,)),
            dma((owners,)), dma((owners,)),
            dma((nc,)), dma((nc,)),
            dma((total,)), dma((total,)),
        ],
        compiler_params=pltpu.CompilerParams(
            collective_id=0, has_side_effects=True, vmem_limit_bytes=40 * 1024 * 1024
        ),
    )(
        tile_count,
        sector_ids.reshape(nq, 128),
        observed,
        weights,
        coefficients,
        tile_index,
        sensitivity.reshape(flat, width),
    )


def solution(mesh):
    placed = (
        P(("parts", "track", "tm")),
        P(None, ("parts", "track", "tm")),
        P(None, ("parts", "track", "tm")),
        P(("parts", "track"), None),
        P(("parts", "track", "tm"), "coef"),
        P(("parts", "track", "tm")),
        P(("parts", "track", "tm"), "coef", None, None, None),
    )
    return jax.shard_map(
        per_device,
        mesh=mesh,
        in_specs=placed,
        out_specs=P(("parts", "track"), None),
        check_vma=False,
    )
```

time: 136 us -> 35.9 us (0.26)
  waiting for transfers between devices: 55.2 us -> 0 us
  Pallas kernels: 0 us -> 28.1 us
  blocking collectives: 17.8 us -> 0 us
  between operations: 13.5 us -> 0.02 us
  starting transfers between devices: 13.1 us -> 0 us
  local copies, waits for them, and re-layouts: 18.6 us -> 7.34 us
  other arithmetic: 10.2 us -> 0 us
  matrix products: 6.73 us -> 0 us
    psum x1 -> x0, waiting for transfers between devices: 32 us -> none  [per_device(): gradient = lax.psum(summed, ('tm', 'coef'))]
    pallas_call x0 -> x1, Pallas kernels: none -> 28.1 us  [per_device(): pl.pallas_call(functools.partial(kernel, (nt, nm, nc, ns, hk, lr)), out_s...]
    reduce_scatter x1 -> x0, waiting for transfers between devices: 19.6 us -> none  [per_device(): lax.psum_scatter(partial_grad, 'track', scatter_dimension=0, tiled=True)]
    all_gather x1 -> x0, blocking collectives: 14.5 us -> none  [per_device(): every_block = lax.all_gather(rounded, 'track', axis=0, tiled=True)]
    all_to_all x2 -> x0, starting transfers between devices: 13 us -> none  [the longest x1 7.25 us: per_device(): lax.all_to_all(labels, ('track', 'tm'), split_axis=0, concat_axis=0, tile...]
    scatter x3 -> x0, local copies, waits for them, and re-layouts: 12.2 us -> none  [the longest x1 4.45 us: per_device(): jnp.zeros((6, sector_total * slot_count + 1), jnp.float32).at[:, target]]
    dot_general x2 -> x0, matrix products: 6.73 us -> none  [the longest x1 3.66 us: per_device(): jnp.einsum('skcjb,skb->scj', sensitivity, blocks, preferred_element_type=...]
    unnamed x1 -> x15, local copies, waits for them, and re-layouts: 1.57 us -> 7.34 us
  transfers between devices with their start and end apart: 4 -> 0, of which waited for: 3 -> 0; matrix products, arithmetic and copies ran while one was open for 13% -> 0% of each run, Pallas kernels for 0% -> 0%
where the time goes in v1:
time: 35.9 us; the launch traced here: 35.5 us
  Pallas kernels  28.1 us (78%)
  local copies, waits for them, and re-layouts  7.34 us (20%)
    pallas_call x1, Pallas kernels, per_device(): pl.pallas_call(functools.partial(kernel, (nt, nm, nc, ns, hk, lr)), out_s...  28.1 us
    unnamed x15, local copies, waits for them, and re-layouts  7.34 us

profile of v1, /device:TPU:0, one launch (start us, length us, event | category | flops | bytes accessed | tf_op | source)
XLA Modules:
  0.0 35.5 jit_solution(8975937267674152472)
XLA Ops:
  0.0 0.0 copy-start
  0.0 2.3 %copy-done = bf16[8,6,3,128,128]{4,3,2,1,0:T(8,128)(2,1)S(1)} copy-done((bf16[8,6,3,128,128]{4,3,2,1,0:T(8,128)(2,1)S(1)}, bf16[8,6,3,128,128]{4,3,2,1,0:T(8,128)(2,1)}, u32[]{:S(2)}) %copy-start) | copy-done | bytes 4718616
  2.3 0.0 copy-start.1
  2.3 0.9 %copy-done.1 = f32[256,128]{1,0:T(8,128)S(1)} copy-done((f32[256,128]{1,0:T(8,128)S(1)}, f32[256,128]{1,0:T(8,128)}, u32[]{:S(2)}) %copy-start.1) | copy-done | bytes 131096
  3.2 0.0 copy-start.2
  3.2 0.7 %copy-done.2 = f32[3,768]{1,0:T(4,128)S(1)} copy-done((f32[3,768]{1,0:T(4,128)S(1)}, f32[3,768]{1,0:T(4,128)}, u32[]{:S(2)}) %copy-start.2) | copy-done | bytes 9240
  4.0 0.0 copy-start.3
  4.0 0.7 %copy-done.3 = f32[3,768]{1,0:T(4,128)S(1)} copy-done((f32[3,768]{1,0:T(4,128)S(1)}, f32[3,768]{1,0:T(4,128)}, u32[]{:S(2)}) %copy-start.3) | copy-done | bytes 9240
  4.7 0.0 copy-start.4
  4.7 0.7 %copy-done.4 = s32[768]{0:T(1024)S(1)} copy-done((s32[768]{0:T(1024)S(1)}, s32[768]{0:T(1024)}, u32[]{:S(2)}) %copy-start.4) | copy-done | bytes 3096
  5.3 0.0 copy-start.5
  5.3 0.7 %copy-done.5 = s32[8,6]{1,0:T(8,128)S(1)} copy-done((s32[8,6]{1,0:T(8,128)S(1)}, s32[8,6]{1,0:T(8,128)}, u32[]{:S(2)}) %copy-start.5) | copy-done | bytes 216
  6.0 0.0 copy-start.6
  6.0 0.7 %copy-done.6 = s32[8]{0:T(128)S(1)} copy-done((s32[8]{0:T(128)S(1)}, s32[8]{0:T(128)}, u32[]{:S(2)}) %copy-start.6) | copy-done | bytes 56
  6.7 28.1 %shard_map.73 = f32[256,128]{1,0:T(8,128)S(1)} custom-call(s32[8]{0:T(128)S(1)} %copy-done.6, s32[6,128]{1,0:T(8,128)S(1)} %bitcast.3, f32[3,768]{1,0:T(4,128)S(1)} %copy-done.2, f32[3,768]{1,0:T(4,128)S(1)} %copy-done.3, f32[256,128]{1,0:T(8,128)S(1)} %copy-done.1, s32[8,6]{1,0:T(8,128)S(1)} %copy-done.5, bf16[18432,128]{1,0:T(8,128)(2,1)S(1)} %bitcast.2), custom_call_target="tpu_custom_call" | custom-call | tf_op jit(solution)/shard_map/pallas_call | solution.py:284
  34.8 0.7 %copy.9 = f32[256,128]{1,0:T(8,128)} copy(f32[256,128]{1,0:T(8,128)S(1)} %shard_map.73) | data formatting | bytes 262144
Async XLA Ops:
  0.0 2.3 %copy-start = (bf16[8,6,3,128,128]{4,3,2,1,0:T(8,128)(2,1)S(1)}, bf16[8,6,3,128,128]{4,3,2,1,0:T(8,128)(2,1)}, u32[]{:S(2)}) copy-start(bf16[8,6,3,128,128]{4,3,2,1,0:T(8,128)(2,1)} %param.13) | copy-start | bytes 14155780
  2.3 0.9 %copy-start.1 = (f32[256,128]{1,0:T(8,128)S(1)}, f32[256,128]{1,0:T(8,128)}, u32[]{:S(2)}) copy-start(f32[256,128]{1,0:T(8,128)} %coef_ref.1) | copy-start | bytes 393220
  3.2 0.7 %copy-start.2 = (f32[3,768]{1,0:T(4,128)S(1)}, f32[3,768]{1,0:T(4,128)}, u32[]{:S(2)}) copy-start(f32[3,768]{1,0:T(4,128)} %obs_ref.1) | copy-start | bytes 27652
  4.0 0.7 %copy-start.3 = (f32[3,768]{1,0:T(4,128)S(1)}, f32[3,768]{1,0:T(4,128)}, u32[]{:S(2)}) copy-start(f32[3,768]{1,0:T(4,128)} %wts_ref.1) | copy-start | bytes 27652
  4.7 0.7 %copy-start.4 = (s32[768]{0:T(1024)S(1)}, s32[768]{0:T(1024)}, u32[]{:S(2)}) copy-start(s32[768]{0:T(1024)} %param.7) | copy-start | bytes 9220
  5.3 0.7 %copy-start.5 = (s32[8,6]{1,0:T(8,128)S(1)}, s32[8,6]{1,0:T(8,128)}, u32[]{:S(2)}) copy-start(s32[8,6]{1,0:T(8,128)} %tile_ref.1) | copy-start | bytes 580
  6.0 0.7 %copy-start.6 = (s32[8]{0:T(128)S(1)}, s32[8]{0:T(128)}, u32[]{:S(2)}) copy-start(s32[8]{0:T(128)} %count_ref.1) | copy-start | bytes 100

commit v2 on v1

v2 whole, which is shorter than its diff:
```python
import functools

import jax
import jax.numpy as jnp
from jax import lax
from jax.experimental import pallas as pl
from jax.experimental.pallas import tpu as pltpu
from jax.sharding import PartitionSpec as P

HUBER = 2.0
F32 = jnp.float32
BF16 = jnp.bfloat16
NT = (((1,), (1,)), ((), ()))
NN = (((1,), (0,)), ((), ()))


def dot(a, b, dims=NN):
    return lax.dot_general(a, b, dims, preferred_element_type=F32)


def iota(shape, dim):
    return lax.broadcasted_iota(jnp.int32, shape, dim)


def wrap(value, size):
    return lax.rem(value, size)


def kernel(
    dims, count_hbm, sid_hbm, obs_hbm, wts_hbm, coef_hbm, tile_hbm, sens_hbm, out_ref,
    count_ref, sid_ref, obs_ref, wts_ref, coef_ref, tile_ref,
    sens, asks, asked, answers, answered, outgoing, rows, preds, gsend, grecv,
    small_sem, sens_sem, ask_send, ask_recv, answer_send, answer_recv,
    row_send, row_recv, pred_send, pred_recv, grad_send, grad_recv,
):
    nt, nm, nc, ns, hk, lr, nh = dims
    owners, total = nt * nm, nt * nm * nc
    slots = 128
    per = coef_ref.shape[0]
    nq = sid_ref.shape[0]
    entries = ns * hk
    wide = nt * lr
    t, m, c = lax.axis_index("track"), lax.axis_index("tm"), lax.axis_index("coef")
    own = t * nm + m
    me = own * nc + c
    mesh_ids = pl.DeviceIdType.MESH

    def each(act, tms, coefs):
        @pl.loop(1, nt)
        def _(dt):
            for dm in range(tms):
                for dc in range(coefs):
                    act(dt, dm, dc)

        for dm in range(tms):
            for dc in range(coefs):
                if dm or dc:
                    act(0, dm, dc)

    def peer(dt, dm, dc):
        return wrap(t + dt, nt), wrap(m + dm, nm), wrap(c + dc, nc)

    def device(at):
        return {"track": at[0], "tm": at[1], "coef": at[2]}

    pairs = (
        (tile_hbm, tile_ref), (count_hbm, count_ref), (sid_hbm, sid_ref), (obs_hbm, obs_ref),
        (wts_hbm, wts_ref), (coef_hbm, coef_ref),
    )
    small = [
        pltpu.make_async_copy(source, target, small_sem.at[i])
        for i, (source, target) in enumerate(pairs)
    ]
    for load in small:
        load.start()
    barrier = pltpu.get_barrier_semaphore()

    def greet(dt, dm, dc):
        pl.semaphore_signal(
            barrier, inc=1, device_id=device(peer(dt, dm, dc)), device_id_type=mesh_ids
        )

    each(greet, nm, nc)
    sector_rows = hk * 3 * slots
    loads = [
        pltpu.make_async_copy(
            sens_hbm.at[pl.ds(s * sector_rows, sector_rows)],
            sens.at[pl.ds(s * sector_rows, sector_rows)],
            sens_sem.at[s],
        )
        for s in range(ns)
    ]
    for load in loads:
        load.start()

    def ask_copy(dt, source):
        at = peer(dt, 0, 0)
        return pltpu.make_async_remote_copy(
            src_ref=asks.at[at[0]], dst_ref=asked.at[source],
            send_sem=ask_send.at[dt], recv_sem=ask_recv.at[source],
            device_id=device(at), device_id_type=mesh_ids,
        )

    def answer_copy(dt, source):
        at = peer(dt, 0, 0)
        return pltpu.make_async_remote_copy(
            src_ref=answers.at[pl.ds(pl.multiple_of(at[0] * lr, lr), lr)],
            dst_ref=answered.at[pl.ds(pl.multiple_of(source * lr, lr), lr)],
            send_sem=answer_send.at[dt], recv_sem=answer_recv.at[source],
            device_id=device(at), device_id_type=mesh_ids,
        )

    def row_copy(dt, dm, source):
        at = peer(dt, dm, 0)
        return pltpu.make_async_remote_copy(
            src_ref=outgoing.at[at[0] * nm + at[1]], dst_ref=rows.at[source],
            send_sem=row_send.at[dt * nm + dm], recv_sem=row_recv.at[source],
            device_id=device(at), device_id_type=mesh_ids,
        )

    def pred_copy(dc, source):
        return pltpu.make_async_remote_copy(
            src_ref=preds.at[c], dst_ref=preds.at[source],
            send_sem=pred_send.at[dc], recv_sem=pred_recv.at[source],
            device_id=device(peer(0, 0, dc)), device_id_type=mesh_ids,
        )

    def grad_copy(dt, dm, dc, source):
        at = peer(dt, dm, dc)
        return pltpu.make_async_remote_copy(
            src_ref=gsend.at[pl.ds(pl.multiple_of(at[0] * lr, lr), lr)], dst_ref=grecv.at[source],
            send_sem=grad_send.at[(dt * nm + dm) * nc + dc], recv_sem=grad_recv.at[source],
            device_id=device(at), device_id_type=mesh_ids,
        )

    small[0].wait()
    small[1].wait()
    index = jnp.concatenate([tile_ref[:, pl.ds(k, 1)] for k in range(hk)], axis=0)
    sub = iota((ns, 1), 0)
    count = jnp.zeros((ns, 1), jnp.int32)
    for s in range(ns):
        count = jnp.where(sub == s, count_ref[s], count)
    active = jnp.concatenate(
        [jnp.where(c * hk + k < count, 1.0, 0.0) for k in range(hk)], axis=0
    )
    lane = iota((entries, 128), 1)
    named = (index >= lane * per) & (index < (lane + 1) * per)
    named_f = jnp.where(named, 1.0, 0.0)
    before = jnp.where(iota((entries, entries), 1) < iota((entries, entries), 0), 1.0, 0.0)
    rank = jnp.sum(dot(before.astype(BF16), named_f.astype(BF16)) * named_f, axis=1, keepdims=True)
    track = jnp.sum(jnp.where(named, lane, 0).astype(F32), axis=1, keepdims=True)
    within = index.astype(F32) - track * per + 1.0
    across = iota((entries, wide), 1).astype(F32)
    mine = (t * lr).astype(F32)
    for u in range(nt):
        asks[u] = jnp.sum(
            jnp.where((track == u) & (rank + mine == across), within, 0.0), axis=0, keepdims=True
        )
    lane_f = lane.astype(F32)
    shift = (lax.rem(me, 128 // lr) * lr).astype(F32)
    marks = []
    for u in range(nt):
        marks.append(
            jnp.sum(
                jnp.where((track == u) & (rank + shift == lane_f), within, 0.0), axis=0, keepdims=True
            )
        )
    spread = jnp.where(track * lr + rank == across, 1.0, 0.0)
    squeeze = spread.T.astype(BF16)
    pick = jnp.where(active > 0.5, spread, 0.0).astype(BF16)
    asked[t] = asks[t]
    pl.semaphore_wait(barrier, total - 1)

    @pl.loop(1, nt)
    def _(dt):
        ask_copy(dt, t).start()

    for load in small[2:5]:
        load.wait()
    ri, rj = iota((128, 256), 0), iota((128, 256), 1)
    tri = jnp.where((ri < rj) | (rj >= 128), 1.0, 0.0).astype(BF16)
    slot_at = iota((slots, 128), 0).astype(F32)
    owner_at = iota((owners, 128), 0) * ns
    first = owner_at.astype(F32)
    key_at = iota((owners * nh, 128), 0).astype(F32)
    ids = [sid_ref[pl.ds(q, 1), :].astype(F32) for q in range(nq)]
    belongs = [jnp.where((i >= first) & (i < first + ns), 1.0, 0.0) for i in ids]
    ahead = dot(jnp.concatenate(belongs, axis=0).astype(BF16), tri)
    base = jnp.zeros((owners, 128), F32)
    high, low, put = [], [], []
    for q in range(nq):
        hit = belongs[q]
        order = ahead[q * owners:(q + 1) * owners, :128] + base
        base = base + ahead[q * owners:(q + 1) * owners, 128:]
        order = jnp.sum(hit * order, axis=0, keepdims=True)
        to = jnp.sum(hit * first, axis=0, keepdims=True)
        half = jnp.zeros_like(order)
        for h in range(1, nh):
            half = half + jnp.where(order >= h * 128.0, 1.0, 0.0)
        key = to * (nh / ns) + half
        put.append(jnp.where(order - half * 128.0 == slot_at, 1.0, 0.0).astype(BF16))
        lanes = pl.ds(q * 128, 128)
        piece = jnp.concatenate(
            [obs_ref[:, lanes], wts_ref[:, lanes], ids[q] - to + 1.0, jnp.zeros((1, 128), F32)], axis=0
        )
        upper = piece.astype(BF16).astype(F32)
        lower = piece - upper
        chosen = jnp.where(key == key_at, 1.0, 0.0)
        high.append(
            jnp.concatenate([chosen[i:i + 1] * upper for i in range(owners * nh)], axis=0).astype(BF16)
        )
        low.append(
            jnp.concatenate([chosen[i:i + 1] * lower for i in range(owners * nh)], axis=0).astype(BF16)
        )
    put = jnp.concatenate(put, axis=1)
    sorted_rows = dot(jnp.concatenate(high, axis=1), put, NT)
    sorted_rows = sorted_rows + dot(jnp.concatenate(low, axis=1), put, NT)
    outgoing[...] = sorted_rows.reshape(owners, nh * 8, 128)
    rows[own] = outgoing[own]

    @pl.loop(1, nt)
    def _(dt):
        ask_copy(0, wrap(t + dt, nt)).wait_recv()

    small[5].wait()
    wanted = asked[0]
    for u in range(1, nt):
        wanted = wanted + asked[u]
    wanted = jnp.broadcast_to(wanted, (128, wide)).T
    per_lane = iota((wide, 128), 1).astype(F32) + 1.0
    chosen = jnp.concatenate(
        [
            jnp.where(wanted == per_lane + (i * 128.0), 1.0, 0.0).astype(BF16)
            for i in range((per + 127) // 128)
        ],
        axis=1,
    )
    if per % 128:
        chosen = chosen[:, :per]
    answers[...] = dot(chosen, coef_ref[...].astype(BF16)).astype(BF16)

    @pl.loop(1, nt)
    def _(dt):
        answer_copy(dt, t).start()

    def send_rows(dt, dm, dc):
        row_copy(dt, dm, own).start()

    each(send_rows, nm, 1)
    own_answer = pl.ds(pl.multiple_of(t * lr, lr), lr)
    answered[own_answer] = answers[own_answer]

    @pl.loop(1, nt)
    def _(dt):
        answer_copy(0, wrap(t + dt, nt)).wait_recv()

    blocks = dot(pick, answered[...])
    wide_blocks = jnp.concatenate(
        [blocks[k * ns:(k + 1) * ns] for k in range(hk)], axis=1
    ).astype(BF16)
    pixels = 3 * slots

    def tile(s, k):
        return sens[pl.ds((s * hk + k) * pixels, pixels), :]

    which = iota((ns, pixels), 0)
    pred = jnp.zeros((ns, pixels), F32)
    for s in range(ns):
        loads[s].wait()
        part = dot(wide_blocks, jnp.concatenate([tile(s, k) for k in range(hk)], axis=1), NT)
        pred = jnp.where(which == s, part, pred)
    preds[c] = pred

    @pl.loop(1, nc)
    def _(dc):
        pred_copy(dc, c).start()

    def take_rows(dt, dm, dc):
        at = peer(dt, dm, 0)
        row_copy(0, 0, at[0] * nm + at[1]).wait_recv()

    each(take_rows, nm, 1)

    sector = iota((ns, 128), 0).astype(F32) + 1.0
    group = min(owners, 8)

    def source_rows(step, carry):
        base, grid = carry
        got = [rows[step * group + j] for j in range(group)]
        pieces = [part[q * 8:(q + 1) * 8] for part in got for q in range(nh)]
        hits = [jnp.where(piece[6:7] == sector, 1.0, 0.0) for piece in pieces]
        ahead = dot(jnp.concatenate(hits, axis=0).astype(BF16), tri)
        put, high, low = [], [], []
        for q, (hit, piece) in enumerate(zip(hits, pieces)):
            rank_q = ahead[q * ns:(q + 1) * ns, :128] + base
            base = base + ahead[q * ns:(q + 1) * ns, 128:]
            slot = jnp.sum(hit * rank_q, axis=0, keepdims=True)
            put.append(jnp.where(slot == slot_at, 1.0, 0.0).astype(BF16))
            chunk = jnp.concatenate([hit * piece[i:i + 1] for i in range(6)], axis=0)
            upper = chunk.astype(BF16)
            high.append(upper)
            low.append((chunk - upper.astype(F32)).astype(BF16))
        both = jnp.concatenate(
            [jnp.concatenate(high, axis=1), jnp.concatenate(low, axis=1)], axis=0
        )
        return base, grid + dot(both, jnp.concatenate(put, axis=1), NT)

    carry = (jnp.zeros((ns, 128), F32), jnp.zeros((12 * ns, slots), F32))
    if owners == group:
        _, grid = source_rows(0, carry)
    else:
        _, grid = lax.fori_loop(0, owners // group, source_rows, carry)
    grid = grid[:6 * ns] + grid[6 * ns:]

    @pl.loop(1, nc)
    def _(dc):
        pred_copy(0, wrap(c + dc, nc)).wait_recv()

    pred = preds[0]
    for i in range(1, nc):
        pred = pred + preds[i]
    forces = []
    for i in range(3):
        w = grid[(3 + i) * ns:(4 + i) * ns]
        scaled = w * (pred[:, i * slots:(i + 1) * slots] - grid[i * ns:(i + 1) * ns])
        forces.append(w * scaled * lax.rsqrt(1.0 + (scaled / HUBER) ** 2))
    force = jnp.concatenate(forces, axis=1).astype(BF16)
    which = iota((ns, hk * 128), 0)
    grad = jnp.zeros((ns, hk * 128), F32)
    for s in range(ns):
        part = dot(force, jnp.concatenate([tile(s, k) for k in range(hk)], axis=1))
        grad = jnp.where(which == s, part, grad)
    grad = jnp.concatenate([grad[:, k * 128:(k + 1) * 128] for k in range(hk)], axis=0)
    grad = jnp.where(active > 0.5, grad, 0.0).astype(BF16)
    packed = dot(squeeze, grad)
    line = iota((nt * lr, 128), 0)
    for u in range(nt):
        packed = jnp.where(line == u * lr + lr - 1, marks[u], packed)
    gsend[...] = packed.astype(BF16)
    grecv[me] = gsend[pl.ds(pl.multiple_of(t * lr, lr), lr)]

    def send_grads(dt, dm, dc):
        grad_copy(dt, dm, dc, me).start()

    each(send_grads, nm, nc)

    def take_grads(dt, dm, dc):
        at = peer(dt, dm, dc)
        grad_copy(0, 0, 0, (at[0] * nm + at[1]) * nc + at[2]).wait_recv()

    each(take_grads, nm, nc)

    together = 128 // lr
    at = iota((per, 128), 0).astype(F32) + 1.0

    def gather_group(g, acc):
        base = g * together
        mark = jnp.zeros((1, 128), F32)
        for i in range(together):
            mark = mark + grecv[base + i].astype(F32)[lr - 1:lr]
        terms = jnp.concatenate([grecv[base + i] for i in range(together)], axis=0)
        return acc + dot(jnp.where(at == mark, 1.0, 0.0).astype(BF16), terms)

    out_ref[...] = lax.fori_loop(0, total // together, gather_group, jnp.zeros((per, 128), F32))

    @pl.loop(1, nt)
    def _(dt):
        ask_copy(dt, t).wait_send()
        answer_copy(dt, t).wait_send()

    def sent_rows(dt, dm, dc):
        row_copy(dt, dm, own).wait_send()

    each(sent_rows, nm, 1)

    @pl.loop(1, nc)
    def _(dc):
        pred_copy(dc, c).wait_send()

    def sent_grads(dt, dm, dc):
        grad_copy(dt, dm, dc, me).wait_send()

    each(sent_grads, nm, nc)


def per_device(sector_ids, observed, weights, coefficients, tile_index, tile_count, sensitivity):
    nt, nm, nc = lax.axis_size("track"), lax.axis_size("tm"), lax.axis_size("coef")
    ns, hk = tile_index.shape
    per, width = coefficients.shape
    nq = sector_ids.shape[0] // 128
    slots = sensitivity.shape[3]
    owners, total = nt * nm, nt * nm * nc
    cap = 2 * ns * hk // nt
    lr = (cap + 1 + 15) // 16 * 16
    nh = (2 * sector_ids.shape[0] // owners + 127) // 128
    flat = ns * hk * 3 * slots
    vmem = pl.BlockSpec(memory_space=pltpu.VMEM)
    dma = pltpu.SemaphoreType.DMA
    return pl.pallas_call(
        functools.partial(kernel, (nt, nm, nc, ns, hk, lr, nh)),
        out_shape=jax.ShapeDtypeStruct((per, width), F32),
        in_specs=[pl.BlockSpec(memory_space=pltpu.HBM)] * 7,
        out_specs=vmem,
        scratch_shapes=[
            pltpu.SMEM(tile_count.shape, jnp.int32),
            pltpu.VMEM((nq, 128), jnp.int32),
            pltpu.VMEM(observed.shape, F32),
            pltpu.VMEM(weights.shape, F32),
            pltpu.VMEM((per, width), F32),
            pltpu.VMEM(tile_index.shape, jnp.int32),
            pltpu.VMEM((flat, width), BF16),
            pltpu.VMEM((nt, 1, nt * lr), F32),
            pltpu.VMEM((nt, 1, nt * lr), F32),
            pltpu.VMEM((nt * lr, width), BF16),
            pltpu.VMEM((nt * lr, width), BF16),
            pltpu.VMEM((owners, nh * 8, 128), F32),
            pltpu.VMEM((owners, nh * 8, 128), F32),
            pltpu.VMEM((nc, ns, 3 * slots), F32),
            pltpu.VMEM((nt * lr, width), BF16),
            pltpu.VMEM((total, lr, width), BF16),
            dma((6,)), dma((ns,)),
            dma((nt,)), dma((nt,)),
            dma((nt,)), dma((nt,)),
            dma((owners,)), dma((owners,)),
            dma((nc,)), dma((nc,)),
            dma((total,)), dma((total,)),
        ],
        compiler_params=pltpu.CompilerParams(
            collective_id=0, has_side_effects=True, vmem_limit_bytes=64 * 1024 * 1024
        ),
    )(
        tile_count,
        sector_ids.reshape(nq, 128),
        observed,
        weights,
        coefficients,
        tile_index,
        sensitivity.reshape(flat, width),
    )


def solution(mesh):
    placed = (
        P(("parts", "track", "tm")),
        P(None, ("parts", "track", "tm")),
        P(None, ("parts", "track", "tm")),
        P(("parts", "track"), None),
        P(("parts", "track", "tm"), "coef"),
        P(("parts", "track", "tm")),
        P(("parts", "track", "tm"), "coef", None, None, None),
    )
    return jax.shard_map(
        per_device,
        mesh=mesh,
        in_specs=placed,
        out_specs=P(("parts", "track"), None),
        check_vma=False,
    )
```

time: 35.9 us -> 25.5 us (0.71)
  local copies, waits for them, and re-layouts: 7.34 us -> 1.57 us
  Pallas kernels: 28.1 us -> 23.7 us
    unnamed x15 -> x1, local copies, waits for them, and re-layouts: 7.34 us -> 1.57 us
    pallas_call x1, Pallas kernels: 28.1 us -> 23.7 us  [per_device(): pl.pallas_call(functools.partial(kernel, (nt, nm, nc, ns, hk, lr, nh)), o...]
where the time goes in v2:
time: 25.5 us; the launch traced here: 25.3 us
  Pallas kernels  23.7 us (93%)
  local copies, waits for them, and re-layouts  1.57 us (6%)
    pallas_call x1, Pallas kernels, per_device(): pl.pallas_call(functools.partial(kernel, (nt, nm, nc, ns, hk, lr, nh)), o...  23.7 us
    unnamed x1, local copies, waits for them, and re-layouts  1.57 us

profile of v2, /device:TPU:0, one launch (start us, length us, event | category | flops | bytes accessed | tf_op | source)
XLA Modules:
  0.0 25.3 jit_solution(8821298260923778297)
XLA Ops:
  0.0 23.7 %shard_map.73 = f32[256,128]{1,0:T(8,128)} custom-call(s32[8]{0:T(128)} %count_hbm.1, s32[6,128]{1,0:T(8,128)} %bitcast.3, f32[3,768]{1,0:T(4,128)} %obs_hbm.1, f32[3,768]{1,0:T(4,128)} %wts_hbm.1, f32[256,128]{1,0:T(8,128)} %coef_hbm.1, s32[8,6]{1,0:T(8,128)} %tile_hbm.1, bf16[18432,128]{1,0:T(8,128)(2,1)} %bitcast.2), custom_call_target="tpu_custom_call" | custom-call | tf_op jit(solution)/shard_map/pallas_call | solution.py:399
  23.7 1.6 %copy.9 = f32[256,128]{1,0:T(8,128)} copy(f32[256,128]{1,0:T(8,128)} %shard_map.73) | data formatting | bytes 262144

commit v3 on v2

--- a/solution.py
+++ b/solution.py
@@ -134,15 +134,7 @@
         )
 
     small[0].wait()
-    small[1].wait()
     index = jnp.concatenate([tile_ref[:, pl.ds(k, 1)] for k in range(hk)], axis=0)
-    sub = iota((ns, 1), 0)
-    count = jnp.zeros((ns, 1), jnp.int32)
-    for s in range(ns):
-        count = jnp.where(sub == s, count_ref[s], count)
-    active = jnp.concatenate(
-        [jnp.where(c * hk + k < count, 1.0, 0.0) for k in range(hk)], axis=0
-    )
     lane = iota((entries, 128), 1)
     named = (index >= lane * per) & (index < (lane + 1) * per)
     named_f = jnp.where(named, 1.0, 0.0)
@@ -156,18 +148,6 @@
         asks[u] = jnp.sum(
             jnp.where((track == u) & (rank + mine == across), within, 0.0), axis=0, keepdims=True
         )
-    lane_f = lane.astype(F32)
-    shift = (lax.rem(me, 128 // lr) * lr).astype(F32)
-    marks = []
-    for u in range(nt):
-        marks.append(
-            jnp.sum(
-                jnp.where((track == u) & (rank + shift == lane_f), within, 0.0), axis=0, keepdims=True
-            )
-        )
-    spread = jnp.where(track * lr + rank == across, 1.0, 0.0)
-    squeeze = spread.T.astype(BF16)
-    pick = jnp.where(active > 0.5, spread, 0.0).astype(BF16)
     asked[t] = asks[t]
     pl.semaphore_wait(barrier, total - 1)
 
@@ -247,6 +227,26 @@
         row_copy(dt, dm, own).start()
 
     each(send_rows, nm, 1)
+    small[1].wait()
+    sub = iota((ns, 1), 0)
+    count = jnp.zeros((ns, 1), jnp.int32)
+    for s in range(ns):
+        count = jnp.where(sub == s, count_ref[s], count)
+    active = jnp.concatenate(
+        [jnp.where(c * hk + k < count, 1.0, 0.0) for k in range(hk)], axis=0
+    )
+    lane_f = lane.astype(F32)
+    shift = (lax.rem(me, 128 // lr) * lr).astype(F32)
+    marks = []
+    for u in range(nt):
+        marks.append(
+            jnp.sum(
+                jnp.where((track == u) & (rank + shift == lane_f), within, 0.0), axis=0, keepdims=True
+            )
+        )
+    spread = jnp.where(track * lr + rank == across, 1.0, 0.0)
+    squeeze = spread.T.astype(BF16)
+    pick = jnp.where(active > 0.5, spread, 0.0).astype(BF16)
     own_answer = pl.ds(pl.multiple_of(t * lr, lr), lr)
     answered[own_answer] = answers[own_answer]
 
@@ -255,9 +255,7 @@
         answer_copy(0, wrap(t + dt, nt)).wait_recv()
 
     blocks = dot(pick, answered[...])
-    wide_blocks = jnp.concatenate(
-        [blocks[k * ns:(k + 1) * ns] for k in range(hk)], axis=1
-    ).astype(BF16)
+    ones = jnp.ones((ns, 256), BF16)
     pixels = 3 * slots
 
     def tile(s, k):
@@ -267,7 +265,12 @@
     pred = jnp.zeros((ns, pixels), F32)
     for s in range(ns):
         loads[s].wait()
-        part = dot(wide_blocks, jnp.concatenate([tile(s, k) for k in range(hk)], axis=1), NT)
+        terms = sum(
+            tile(s, k).astype(F32) * blocks[k * ns + s:k * ns + s + 1] for k in range(hk)
+        )
+        upper = terms.astype(BF16)
+        lower = (terms - upper.astype(F32)).astype(BF16)
+        part = dot(ones, jnp.concatenate([upper, lower], axis=1), NT)
         pred = jnp.where(which == s, part, pred)
     preds[c] = pred
 
@@ -353,15 +356,23 @@
     together = 128 // lr
     at = iota((per, 128), 0).astype(F32) + 1.0
 
-    def gather_group(g, acc):
-        base = g * together
-        mark = jnp.zeros((1, 128), F32)
-        for i in range(together):
-            mark = mark + grecv[base + i].astype(F32)[lr - 1:lr]
-        terms = jnp.concatenate([grecv[base + i] for i in range(together)], axis=0)
-        return acc + dot(jnp.where(at == mark, 1.0, 0.0).astype(BF16), terms)
-
-    out_ref[...] = lax.fori_loop(0, total // together, gather_group, jnp.zeros((per, 128), F32))
+    bundle = min(total // together, 4)
+
+    def gather_groups(step, acc):
+        finds, terms = [], []
+        for g in range(bundle):
+            base = (step * bundle + g) * together
+            parts = [grecv[base + i] for i in range(together)]
+            mark = sum(part.astype(F32)[lr - 1:lr] for part in parts)
+            finds.append(jnp.where(at == mark, 1.0, 0.0).astype(BF16))
+            terms.extend(parts)
+        return acc + dot(jnp.concatenate(finds, axis=1), jnp.concatenate(terms, axis=0))
+
+    acc = jnp.zeros((per, 128), F32)
+    if total == bundle * together:
+        out_ref[...] = gather_groups(0, acc)
+    else:
+        out_ref[...] = lax.fori_loop(0, total // (bundle * together), gather_groups, acc)
 
     @pl.loop(1, nt)
     def _(dt):

time: 25.5 us -> 24.7 us (0.969)
  Pallas kernels: 23.7 us -> 22.9 us
    pallas_call x1, Pallas kernels: 23.7 us -> 22.9 us  [per_device(): pl.pallas_call(functools.partial(kernel, (nt, nm, nc, ns, hk, lr, nh)), o...]
where the time goes in v3:
time: 24.7 us; the launch traced here: 24.5 us
  Pallas kernels  22.9 us (93%)
  local copies, waits for them, and re-layouts  1.57 us (6%)
    pallas_call x1, Pallas kernels, per_device(): pl.pallas_call(functools.partial(kernel, (nt, nm, nc, ns, hk, lr, nh)), o...  22.9 us
    unnamed x1, local copies, waits for them, and re-layouts  1.57 us

profile of v3, /device:TPU:0, one launch (start us, length us, event | category | flops | bytes accessed | tf_op | source)
XLA Modules:
  0.0 24.5 jit_solution(3113841243058205324)
XLA Ops:
  0.0 22.9 %shard_map.73 = f32[256,128]{1,0:T(8,128)} custom-call(s32[8]{0:T(128)} %count_hbm.1, s32[6,128]{1,0:T(8,128)} %bitcast.3, f32[3,768]{1,0:T(4,128)} %obs_hbm.1, f32[3,768]{1,0:T(4,128)} %wts_hbm.1, f32[256,128]{1,0:T(8,128)} %coef_hbm.1, s32[8,6]{1,0:T(8,128)} %tile_hbm.1, bf16[18432,128]{1,0:T(8,128)(2,1)} %bitcast.2), custom_call_target="tpu_custom_call" | custom-call | tf_op jit(solution)/shard_map/pallas_call | solution.py:410
  22.9 1.6 %copy.9 = f32[256,128]{1,0:T(8,128)} copy(f32[256,128]{1,0:T(8,128)} %shard_map.73) | data formatting | bytes 262144
